TPU v7x, 256 devices: a whole 4x4x8 slice. The times are simulated.
256 devices in a mesh: ctx: 32 (over x, y, core), head: 8 (over z).
Axes of the slice: x: 4, y: 4, z: 8, core: 2. Of those that a mesh axis runs over, the one named last changes fastest.
Arguments:
- queries: bfloat16 [8192, 8192], P('ctx', 'head'), may hold values from -9 to 9
- cache_keys: bfloat16 [262144, 1024], P('ctx', 'head'), may hold values from -4.5 to 4.5
- cache_values: bfloat16 [262144, 1024], P('ctx', 'head'), may hold values from -4.5 to 4.5
- span_keys: bfloat16 [8192, 1024], P('ctx', 'head'), may hold values from -4.5 to 4.5
- span_values: bfloat16 [8192, 1024], P('ctx', 'head'), may hold values from -4.5 to 4.5
- selected: int32 [64, 24], replicated, may hold values from 0 to 2047, as said below
- counts: int32 [64], replicated, may hold values from 6 to 24, as said below
- out_weight: bfloat16 [8192, 8192], P('head', 'ctx'), may hold values from -0.0625 to 0.0625
Outputs:
- output: bfloat16 [8192, 8192], P('ctx', 'head')
Inputs may be any that keep to these rules, and one draw needn't show every extreme that they name: `selected`: row b names the cache blocks of query block b. Its first counts[b] entries are distinct; the others are 0. Over the query blocks of one ctx index (blocks c * 2 to c * 2 + 1), at most 2 live entries name blocks of one ctx index's cache (blocks s * 64 to s * 64 + 63), and some pair reaches 2. `counts`: every query block of some ctx index has 24.
All inputs are finite; a program needn't handle non-finite values.
Results may differ from a plain program's by a relative error of at most 0.0057.
Values may be sent and summed in bfloat16 or wider, within the bound.
A program may use at most 128 MiB of HBM per device.

v0:
```python
import math

import jax
import jax.numpy as jnp
from jax import lax
from jax.sharding import PartitionSpec as P

HQ = 64
KVH = 8
HD = 128
BLK = 128


def per_device(
    queries, cache_keys, cache_values, span_keys, span_values, selected, counts, out_weight
):
    ctx_count = lax.axis_size("ctx")
    my_ctx = lax.axis_index("ctx")
    q_rows, q_width = queries.shape
    ctx_rows, kv_width = cache_keys.shape
    kv_heads = kv_width // HD
    q_group = HQ // KVH
    blocks_dev = ctx_rows // BLK
    qblocks_dev = q_rows // BLK
    width_sel = selected.shape[1]
    lap_count = (width_sel + ctx_count - 1) // ctx_count
    capacity = qblocks_dev * lap_count
    entries = qblocks_dev * width_sel
    owners = (selected // blocks_dev).reshape(ctx_count, entries)
    within = (selected % blocks_dev).reshape(ctx_count, entries)
    live_mask = (lax.broadcasted_iota(jnp.int32, selected.shape, 1) < counts[:, None]).reshape(
        ctx_count, entries
    )
    entry_order = jnp.arange(entries, dtype=jnp.int32)
    earlier = entry_order[None, :] < entry_order[:, None]
    same_owner = (
        (owners[:, :, None] == owners[:, None, :]) & live_mask[:, None, :] & earlier[None, :, :]
    )
    slot_rank = jnp.sum(same_owner.astype(jnp.int32), axis=2)
    mine_live = live_mask & (owners == my_ctx)
    slot_ids = jnp.arange(capacity, dtype=jnp.int32)
    slot_hits = mine_live[:, :, None] & (slot_rank[:, :, None] == slot_ids[None, None, :])
    slot_block = jnp.sum(jnp.where(slot_hits, within[:, :, None], 0), axis=1)
    key_blocks = cache_keys.reshape(blocks_dev, BLK, kv_width)
    value_blocks = cache_values.reshape(blocks_dev, BLK, kv_width)
    outgoing = jnp.stack((key_blocks[slot_block], value_blocks[slot_block]), axis=2)
    incoming = lax.all_to_all(outgoing, "ctx", split_axis=0, concat_axis=0, tiled=True)
    incoming = incoming.reshape(ctx_count * capacity, 2, BLK, kv_width)
    own_owner = lax.dynamic_index_in_dim(owners, my_ctx, 0, keepdims=False)
    own_rank = lax.dynamic_index_in_dim(slot_rank, my_ctx, 0, keepdims=False)
    own_live = lax.dynamic_index_in_dim(live_mask, my_ctx, 0, keepdims=False)
    flat_index = jnp.where(own_live, own_owner * capacity + own_rank, 0)
    gathered = incoming[flat_index].reshape(qblocks_dev, width_sel, 2, BLK, kv_width)
    live_keys = jnp.repeat(own_live.reshape(qblocks_dev, width_sel), BLK, axis=1)
    score_scale = 1.0 / math.sqrt(HD)
    causal = lax.broadcasted_iota(jnp.int32, (BLK, BLK), 1) <= lax.broadcasted_iota(
        jnp.int32, (BLK, BLK), 0
    )

    def attend(block_items):
        q_block, picked, key_live, own_keys, own_values = block_items
        q_block = q_block.reshape(BLK, kv_heads, q_group, HD)
        sel_keys = picked[:, 0].reshape(width_sel * BLK, kv_heads, HD)
        sel_values = picked[:, 1].reshape(width_sel * BLK, kv_heads, HD)
        own_keys = own_keys.reshape(BLK, kv_heads, HD)
        own_values = own_values.reshape(BLK, kv_heads, HD)
        s_sel = (
            jnp.einsum("tgrd,kgd->gtrk", q_block, sel_keys, preferred_element_type=jnp.float32)
            * score_scale
        )
        s_sel = jnp.where(key_live[None, None, None, :], s_sel, -jnp.inf)
        s_own = (
            jnp.einsum("tgrd,kgd->gtrk", q_block, own_keys, preferred_element_type=jnp.float32)
            * score_scale
        )
        s_own = jnp.where(causal[None, :, None, :], s_own, -jnp.inf)
        row_max = jnp.maximum(jnp.max(s_sel, axis=-1), jnp.max(s_own, axis=-1))
        p_sel = jnp.exp(s_sel - row_max[..., None])
        p_own = jnp.exp(s_own - row_max[..., None])
        row_sum = jnp.sum(p_sel, axis=-1) + jnp.sum(p_own, axis=-1)
        weighted = jnp.einsum(
            "gtrk,kgd->gtrd",
            p_sel.astype(jnp.bfloat16),
            sel_values,
            preferred_element_type=jnp.float32,
        )
        weighted = weighted + jnp.einsum(
            "gtrk,kgd->gtrd",
            p_own.astype(jnp.bfloat16),
            own_values,
            preferred_element_type=jnp.float32,
        )
        result = weighted / row_sum[..., None]
        return (
            jnp.transpose(result, (1, 0, 2, 3))
            .reshape(BLK, kv_heads * q_group * HD)
            .astype(jnp.bfloat16)
        )

    attention = lax.map(
        attend,
        (
            queries.reshape(qblocks_dev, BLK, q_width),
            gathered,
            live_keys,
            span_keys.reshape(qblocks_dev, BLK, kv_width),
            span_values.reshape(qblocks_dev, BLK, kv_width),
        ),
    ).reshape(q_rows, q_width)
    partial_value = jnp.dot(
        attention,
        lax.all_gather(out_weight, "ctx", axis=1, tiled=True),
        preferred_element_type=jnp.float32,
    )
    return lax.psum_scatter(partial_value, "head", scatter_dimension=1, tiled=True).astype(
        jnp.bfloat16
    )


def solution(mesh):
    placed = (
        P("ctx", "head"),
        P("ctx", "head"),
        P("ctx", "head"),
        P("ctx", "head"),
        P("ctx", "head"),
        P(),
        P(),
        P("head", "ctx"),
    )
    return jax.shard_map(
        per_device, mesh=mesh, in_specs=placed, out_specs=P("ctx", "head"), check_vma=False
    )
```

profile of v0, /device:TPU:3, one launch (start us, length us, event | category | flops | bytes accessed | tf_op | source)
XLA Modules:
  0.0 257.2 jit_solution(8583947223089259556)
XLA Ops:
  6.5 0.7 all-gather.2.cloned.1.call-update
  7.3 0.7 add_select_fusion
  8.1 0.8 lt.76
  9.4 0.9 convert_reduce_fusion
  10.6 2.1 gather_fusion
  12.7 3.9 %gather_fusion.1 = bf16[64,128,128]{2,1,0:T(8,128)(2,1)} fusion(bf16[64,128,128]{2,1,0:T(8,128)(2,1)} %bitcast.85, s32[1024]{0:T(1024)S(1)} %pad_clamp_fusion.1), kind=kCustom, calls=%fused_computation.1 | custom fusion | bytes 4194560 | tf_op jit(solution)/shard_map/gather | solution.py:46
  16.6 3.9 %pad_maximum_fusion = bf16[32,2,2,128,128]{4,3,1,2,0:T(8,128)(2,1)} fusion(bf16[32,2,1,128,128]{4,3,1,2,0:T(8,128)(2,1)} %bitcast.82, bf16[32,2,1,128,128]{4,3,1,2,0:T(8,128)(2,1)S(1)} %bitcast.81), kind=kLoop, calls=%fused_computation.34 | loop fusion | flops 2097152 | bytes 8388608 | tf_op jit(solution)/shard_map/stack | solution.py:46
  20.5 8.0 %all-to-all-start = ((bf16[32,2,2,128,128]{4,3,1,2,0:T(8,128)(2,1)}), bf16[32,2,2,128,128]{4,3,1,2,0:T(8,128)(2,1)}, u32[]{:S(2)}, u32[]{:S(2)}) async-start(bf16[32,2,2,128,128]{4,3,1,2,0:T(8,128)(2,1)} %pad_maximum_fusion), calls=%async_computation | async-start | bytes 8388608 | tf_op jit(solution)/shard_map/all_to_all | solution.py:47
  29.0 54.9 %all-to-all-done = bf16[32,2,2,128,128]{4,3,1,2,0:T(8,128)(2,1)} async-done(((bf16[32,2,2,128,128]{4,3,1,2,0:T(8,128)(2,1)}), bf16[32,2,2,128,128]{4,3,1,2,0:T(8,128)(2,1)}, u32[]{:S(2)}, u32[]{:S(2)}) %all-to-all-start) | async-done | bytes 4194336 | tf_op jit(solution)/shard_map/all_to_all | solution.py:47
  83.9 4.7 %copy.89 = bf16[32,2,2,128,128]{4,3,2,1,0:T(8,128)(2,1)} copy(bf16[32,2,2,128,128]{4,3,1,2,0:T(8,128)(2,1)} %all-to-all-done) | data formatting | bytes 8388608 | tf_op jit(solution)/shard_map/all_to_all | solution.py:47
  88.7 3.4 %gather_fusion.2 = bf16[48,2,128,128]{3,2,1,0:T(8,128)(2,1)S(1)} fusion(bf16[64,2,128,128]{3,2,1,0:T(8,128)(2,1)} %bitcast.80, s32[1024]{0:T(1024)S(1)} %pad_clamp_fusion), kind=kCustom, calls=%fused_computation.2 | custom fusion | bytes 6291648 | tf_op jit(solution)/shard_map/gather | solution.py:53
  92.1 27.8 %while.11 = (s32[]{:T(128)}, bf16[2,128,1024]{2,1,0:T(8,128)(2,1)}, pred[2,3072]{1,0:T(4,128)(4,1)S(1)}, bf16[2,128,1024]{2,1,0:T(8,128)(2,1)}, bf16[2,24,2,128,...) while((s32[]{:T(128)}, bf16[2,128,1024]{2,1,0:T(8,128)(2,1)}, ...), condition=%wide.region_7.8_spmd.clone, body=%wide.region_2.7_spmd.clone.sunk | while | flops 1713649664 | bytes 81702608 | solution.py:100
  92.1 1.6 copy-done.2
  93.9 1.0 fusion.61
  95.1 2.1 fusion.62
  97.6 2.7 %fusion.65 = f32[128,8]{0,1:T(8,128)S(1)} fusion(f32[128,8,3072]{2,0,1:T(8,128)S(1)} %get-tuple-element.174, f32[128,8]{0,1:T(8,128)S(1)} %max.11, pred[3072]{0:T(1024)(128)(4,1)S(1)} %dynamic-slice_reduce_fusion.2), kind=kLoop, calls=%fused_computation.7.clone.1 | loop fusion | flops 12581888 | bytes 12594176 | tf_op jit(solution)/shard_map/while/body/eval_jaxpr/reduce_sum | solution.py:80
  100.3 2.8 %fusion.64 = f32[128,8,128]{0,2,1:T(8,128)S(1)} fusion(bf16[3072,128,1]{1,0,2:T(8,128)(2,1)S(1)} %bitcast.79, f32[128,8,3072]{2,0,1:T(8,128)S(1)} %get-tuple-element.174, f32[128,8]{0,1:T(8,128)S(1)} %max.11, pred[3072]{0:T(1024)(128)(4,1)S(1)} %dynamic-slice_reduce_fusion.2), kind=kOutput, calls=%fused_computation.9.clone.1 | convolution fusion | flops 817889280 | bytes 13900800 | tf_op jit(solution)/shard_map/while/body/eval_jaxpr/gtrk,kgd->gtrd/dot_general | solution.py:81
  103.1 1.0 fusion.67
  104.1 1.1 copy.112
  105.2 0.7 constant_dynamic-update-slice_fusion.2
  106.0 1.6 copy-done.2
  107.8 1.0 fusion.61
  109.0 2.1 fusion.62
  111.5 2.7 %fusion.65 = f32[128,8]{0,1:T(8,128)S(1)} fusion(f32[128,8,3072]{2,0,1:T(8,128)S(1)} %get-tuple-element.174, f32[128,8]{0,1:T(8,128)S(1)} %max.11, pred[3072]{0:T(1024)(128)(4,1)S(1)} %dynamic-slice_reduce_fusion.2), kind=kLoop, calls=%fused_computation.7.clone.1 | loop fusion | flops 12581888 | bytes 12594176 | tf_op jit(solution)/shard_map/while/body/eval_jaxpr/reduce_sum | solution.py:80
  114.2 2.8 %fusion.64 = f32[128,8,128]{0,2,1:T(8,128)S(1)} fusion(bf16[3072,128,1]{1,0,2:T(8,128)(2,1)S(1)} %bitcast.79, f32[128,8,3072]{2,0,1:T(8,128)S(1)} %get-tuple-element.174, f32[128,8]{0,1:T(8,128)S(1)} %max.11, pred[3072]{0:T(1024)(128)(4,1)S(1)} %dynamic-slice_reduce_fusion.2), kind=kOutput, calls=%fused_computation.9.clone.1 | convolution fusion | flops 817889280 | bytes 13900800 | tf_op jit(solution)/shard_map/while/body/eval_jaxpr/gtrk,kgd->gtrd/dot_general | solution.py:81
  117.0 1.0 fusion.67
  118.0 1.1 copy.112
  119.1 0.7 constant_dynamic-update-slice_fusion.2
  119.8 19.5 %all-gather.2.cloned.1.call-done = bf16[1024,8192]{1,0:T(8,128)(2,1)} async-done(((bf16[1024,256]{1,0:T(8,128)(2,1)}), bf16[1024,8192]{1,0:T(8,128)(2,1)}) %all-gather.2.cloned.1.call-update) | async-done | bytes 16777232 | tf_op jit(solution)/shard_map/all_gather | solution.py:112
  139.3 13.7 %fusion.33 = f32[256,8192]{1,0:T(8,128)} fusion(bf16[256,1024]{1,0:T(8,128)(2,1)} %bitcast.86, bf16[1024,8192]{1,0:T(8,128)(2,1)} %all-gather.2.cloned.1.call-done), kind=kOutput, calls=%fused_computation.66 | convolution fusion | flops 4294967296 | bytes 25690112 | tf_op jit(solution)/shard_map/dot_general | solution.py:110
  153.0 95.2 %reduce-scatter.2.cloned.1.call-done = f32[256,1024]{1,0:T(8,128)} async-done(((f32[256,8192]{1,0:T(8,128)}), f32[256,1024]{1,0:T(8,128)}) %reduce-scatter.2.cloned.1.call-update) | async-done | bytes 1048592 | tf_op jit(solution)/shard_map/reduce_scatter | solution.py:115
  248.2 2.1 convert_element_type.28
  (68 shorter events, 2.9 us)
Async XLA Ops:
  6.5 4.0 %copy-start = (bf16[8192,128]{1,0:T(8,128)(2,1)S(1)}, bf16[8192,128]{1,0:T(8,128)(2,1)}, u32[]{:S(2)}) copy-start(bf16[8192,128]{1,0:T(8,128)(2,1)} %param.11) | copy-start | bytes 6291460
  6.5 132.8 %all-gather.2.cloned.1.call-start = ((), (), s32[]{:S(2)}) async-start(), calls=%async_computation.2 | async-start | bytes 17301504 | tf_op jit(solution)/shard_map/all_gather | solution.py:112
  12.7 3.9 %copy-start.5 = (bf16[64,128,128]{2,1,0:T(8,128)(2,1)S(1)}, bf16[64,128,128]{2,1,0:T(8,128)(2,1)}, u32[]{:S(2)}) copy-start(bf16[64,128,128]{2,1,0:T(8,128)(2,1)} %gather_fusion) | copy-start | bytes 6291460
  20.5 63.4 %all-to-all-start = ((bf16[32,2,2,128,128]{4,3,1,2,0:T(8,128)(2,1)}), bf16[32,2,2,128,128]{4,3,1,2,0:T(8,128)(2,1)}, u32[]{:S(2)}, u32[]{:S(2)}) async-start(bf16[32,2,2,128,128]{4,3,1,2,0:T(8,128)(2,1)} %pad_maximum_fusion), calls=%async_computation | async-start | bytes 8388608 | tf_op jit(solution)/shard_map/all_to_all | solution.py:47
  28.5 219.7 %reduce-scatter.2.cloned.1.call-start = ((), (), s32[]{:S(2)}) async-start(), calls=%async_computation.3 | async-start | bytes 9437184 | tf_op jit(solution)/shard_map/reduce_scatter | solution.py:115
  88.6 3.4 %copy-start.7 = (bf16[256,128]{1,0:T(8,128)(2,1)S(1)}, bf16[256,128]{1,0:T(8,128)(2,1)}, u32[]{:S(2)}) copy-start(bf16[256,128]{1,0:T(8,128)(2,1)} %param.13) | copy-start | bytes 196612
  88.6 3.4 %copy-start.8 = (bf16[256,128]{1,0:T(8,128)(2,1)S(1)}, bf16[256,128]{1,0:T(8,128)(2,1)}, u32[]{:S(2)}) copy-start(bf16[256,128]{1,0:T(8,128)(2,1)} %param.14) | copy-start | bytes 196612
  92.1 1.7 copy-start.2
  92.1 2.9 %copy-start.6 = (bf16[2,128,1024]{2,1,0:T(8,128)(2,1)S(1)}, bf16[2,128,1024]{2,1,0:T(8,128)(2,1)}, u32[]{:S(2)}) copy-start(bf16[2,128,1024]{2,1,0:T(8,128)(2,1)} %get-tuple-element.197) | copy-start | bytes 1572868 | tf_op jit(solution)/shard_map/while
  97.6 2.7 %copy-start.4 = (bf16[24,1,128,128]{3,2,0,1:T(8,128)(2,1)S(1)}, bf16[24,1,128,128]{3,2,0,1:T(8,128)(2,1)}, u32[]{:S(2)}) copy-start(bf16[24,1,128,128]{3,2,0,1:T(8,128)(2,1)} %get-tuple-element.172) | copy-start | bytes 2359300 | tf_op jit(solution)/shard_map/while
  100.3 5.6 %copy-start.3 = (bf16[2,24,2,128,128]{4,3,2,1,0:T(8,128)(2,1)S(1)}, bf16[2,24,2,128,128]{4,3,2,1,0:T(8,128)(2,1)}, u32[]{:S(2)}) copy-start(bf16[2,24,2,128,128]{4,3,2,1,0:T(8,128)(2,1)} %copy-done.2) | copy-start | bytes 9437188 | tf_op jit(solution)/shard_map/while
  105.9 1.7 copy-start.2
  105.9 2.9 %copy-start.6 = (bf16[2,128,1024]{2,1,0:T(8,128)(2,1)S(1)}, bf16[2,128,1024]{2,1,0:T(8,128)(2,1)}, u32[]{:S(2)}) copy-start(bf16[2,128,1024]{2,1,0:T(8,128)(2,1)} %get-tuple-element.197) | copy-start | bytes 1572868 | tf_op jit(solution)/shard_map/while
  111.5 2.7 %copy-start.4 = (bf16[24,1,128,128]{3,2,0,1:T(8,128)(2,1)S(1)}, bf16[24,1,128,128]{3,2,0,1:T(8,128)(2,1)}, u32[]{:S(2)}) copy-start(bf16[24,1,128,128]{3,2,0,1:T(8,128)(2,1)} %get-tuple-element.172) | copy-start | bytes 2359300 | tf_op jit(solution)/shard_map/while
  114.2 5.6 %copy-start.3 = (bf16[2,24,2,128,128]{4,3,2,1,0:T(8,128)(2,1)S(1)}, bf16[2,24,2,128,128]{4,3,2,1,0:T(8,128)(2,1)}, u32[]{:S(2)}) copy-start(bf16[2,24,2,128,128]{4,3,2,1,0:T(8,128)(2,1)} %copy-done.2) | copy-start | bytes 9437188 | tf_op jit(solution)/shard_map/while
  153.0 97.3 %copy-start.1 = (bf16[8192,128]{1,0:T(8,128)(2,1)S(1)}, bf16[8192,128]{1,0:T(8,128)(2,1)}, u32[]{:S(2)}) copy-start(bf16[8192,128]{1,0:T(8,128)(2,1)} %param.11) | copy-start | bytes 6291460
Sparse Core Ops, SparseCore 0:
  9.8 129.4 all-gather.1
  153.2 94.9 reduce-scatter.1
where the time goes:
time: 258 us; the launch traced here: 257 us
  waiting for transfers between devices  170 us (66%)
  matrix products  25.9 us (10%)
  local copies, waits for them, and re-layouts  25.6 us (10%)
  between operations  13.5 us (5%)
  other arithmetic  13.4 us (5%)
  starting transfers between devices  8.21 us (3%)
    reduce_scatter x1, waiting for transfers between devices, per_device(): lax.psum_scatter(partial_value, 'head', scatter_dimension=1, tiled=True)  95.2 us
    all_to_all x1, waiting for transfers between devices, per_device(): lax.all_to_all(outgoing, 'ctx', split_axis=0, concat_axis=0, tiled=True)  54.9 us
    all_gather x1, waiting for transfers between devices, per_device(): lax.all_gather(out_weight, 'ctx', axis=1, tiled=True)  19.5 us
    dot_general x1, matrix products, per_device(): jnp.dot(attention, lax.all_gather(out_weight, 'ctx', axis=1, tiled=True),...  13.7 us
    all_to_all x1, starting transfers between devices, per_device(): lax.all_to_all(outgoing, 'ctx', split_axis=0, concat_axis=0, tiled=True)  7.99 us
    reduce_sum x4, other arithmetic, attend(): row_sum = jnp.sum(p_sel, axis=-1) + jnp.sum(p_own, axis=-1)  5.59 us
    dot_general x2, matrix products, attend(): jnp.einsum('gtrk,kgd->gtrd', p_sel.astype(jnp.bfloat16), sel_values, pref...  5.58 us
  transfers between devices with their start and end apart: 3, of which 3 were waited for; matrix products, arithmetic and copies ran while one was open for 18% of the time, Pallas kernels for 0%

commit v1 on v0

v1 whole, which is shorter than its diff:
```python
import functools
import math

import jax
import jax.numpy as jnp
from jax import lax
from jax.experimental import pallas as pl
from jax.experimental.pallas import tpu as pltpu
from jax.sharding import PartitionSpec as P

HD = 128
BLK = 128
SEL = 24
GROUP = 8
NX = 4
NY = 4
NZ = 8
NCTX = 32
CBLK = 64
PAIRS = SEL // 2
MESH = pl.DeviceIdType.MESH
EXP_SCALE = math.log2(math.e) / math.sqrt(HD)

NEAR = [(1, 0), (3, 0), (0, 1), (0, 3)]
DIAG = [(1, 1), (3, 3), (1, 3), (3, 1)]
FAR = [(2, 0), (0, 2), (2, 1), (1, 2), (2, 3), (3, 2), (2, 2)]
KV_ORDER = [(a, b, k) for g in (NEAR, DIAG, FAR) for k in (0, 1) for a, b in g] + [(0, 0, 1)]


def weight_plan():
    plan = {}
    for path in ("a", "b"):
        base = 0 if path == "a" else 512

        def at(u, v, path=path):
            return (u, v) if path == "a" else (v, u)

        for s in (1, -1):
            plan[path, 1, 0, s] = (at(0, 0), base, 512, at(s, 0))
            quarter = base if s == 1 else base + 256
            plan[path, 2, 0, s] = (at(-s, 0), quarter, 256, at(s, 0))
            for u in (0, -1, 1, 2):
                plan[path, 3, u, s] = (at(u, 0), base, 512, at(0, s))
                plan[path, 4, u, s] = (at(u, -s), quarter, 256, at(0, s))
    return plan


PLAN = weight_plan()
PLAN_ID = {name: n for n, name in enumerate(PLAN)}
SIB = {}
for _path in ("a", "b"):
    for _u in range(-1, 3):
        for _v in range(-1, 3):
            if (_u, _v) != (0, 0):
                SIB[_path, _u, _v] = len(SIB) + 1


def body(
    meta, q_hbm, ck_hbm, cv_hbm, sk_hbm, sv_hbm, w_hbm, o_ref,
    kc, vc, qv, skv, svv, outgo, income, wfull, attn, q8, scores, own_scores, mx, lsum, acc,
    load_sem, kv_send, kv_recv, perm_sem, w_send, w_recv, s_send, s_recv, a_send, a_recv,
):
    c = lax.axis_index("ctx")
    z = lax.axis_index("head")
    x = c // 8
    y = (c // 2) % 4
    k = c % 2

    loads = [
        pltpu.make_async_copy(src, dst, load_sem.at[n])
        for n, (src, dst) in enumerate(
            ((ck_hbm, kc), (cv_hbm, vc), (q_hbm, qv), (sk_hbm, skv), (sv_hbm, svv))
        )
    ]
    for cp in loads:
        cp.start()

    def ctx_at(dx, dy, dk=0):
        return ((x + dx + NX) % NX) * 8 + ((y + dy + NY) % NY) * 2 + (k + dk) % 2

    pz = c // 4
    pb = (c // 2) % 2
    perm_to = (4 * ((pz + z) % NZ) + 2 * pb + k, pz)
    perm_from = (4 * z + 2 * pb + k, (pz - z + NZ) % NZ)
    perm_self = (pz == z) & (z == 0)

    barrier = pltpu.get_barrier_semaphore()

    def greet(i, carry):
        pl.semaphore_signal(barrier, inc=1, device_id=((c + i) % NCTX, z), device_id_type=MESH)
        return carry

    lax.fori_loop(1, NCTX, greet, 0)
    for dz in (1, NZ - 1):
        pl.semaphore_signal(barrier, inc=1, device_id=(c, (z + dz) % NZ), device_id_type=MESH)

    @pl.when(jnp.logical_not(perm_self))
    def _():
        pl.semaphore_signal(barrier, inc=1, device_id=perm_to, device_id_type=MESH)
        pl.semaphore_signal(barrier, inc=1, device_id=perm_from, device_id_type=MESH)

    pl.semaphore_wait(barrier, jnp.where(perm_self, NCTX + 1, NCTX + 3))

    def slot(dx, dy, lane=None):
        xy = ((x + dx + NX) % NX) * NY + (y + dy + NY) % NY
        return (xy // 2 - z + NZ) % NZ, 2 * (xy % 2) + (k if lane is None else lane)

    perm_remote = pltpu.make_async_remote_copy(
        src_ref=w_hbm, dst_ref=wfull.at[z, 2 * pb + k], send_sem=perm_sem.at[0],
        recv_sem=perm_sem.at[1], device_id=perm_to, device_id_type=MESH,
    )
    perm_local = pltpu.make_async_copy(w_hbm, wfull.at[z, 2 * pb + k], perm_sem.at[1])

    @pl.when(perm_self)
    def _():
        perm_local.start()

    @pl.when(jnp.logical_not(perm_self))
    def _():
        perm_remote.start()

    loads[0].wait()
    loads[1].wait()

    def kv_copy(d, source):
        return pltpu.make_async_remote_copy(
            src_ref=outgo.at[d], dst_ref=income.at[source], send_sem=kv_send.at[d],
            recv_sem=kv_recv.at[source], device_id=(d, z), device_id_type=MESH,
        )

    for dx, dy, dk in KV_ORDER:
        d = ctx_at(dx, dy, dk)
        for r in range(2):
            blk = meta[2 * d + r]
            outgo[d, r, 0] = kc[blk]
            outgo[d, r, 1] = vc[blk]
        kv_copy(d, c).start()
    for r in range(2):
        blk = meta[2 * c + r]
        income[c, r, 0] = kc[blk]
        income[c, r, 1] = vc[blk]
    loads[2].wait()
    loads[3].wait()
    loads[4].wait()

    def w_copy(name):
        (dx, dy), row, rows, (tx, ty) = PLAN[name]
        zp, bk = slot(dx, dy)
        piece = wfull.at[zp, bk, pl.ds(row, rows)]
        n = PLAN_ID[name]
        return pltpu.make_async_remote_copy(
            src_ref=piece, dst_ref=piece, send_sem=w_send.at[n], recv_sem=w_recv.at[n],
            device_id=(ctx_at(tx, ty), z), device_id_type=MESH,
        )

    def w_arrived(name):
        (dx, dy), row, rows, (tx, ty) = PLAN[name]
        zp, bk = slot(dx - tx, dy - ty)
        piece = wfull.at[zp, bk, pl.ds(row, rows)]
        n = PLAN_ID[name]
        pltpu.make_async_remote_copy(
            src_ref=piece, dst_ref=piece, send_sem=w_send.at[n], recv_sem=w_recv.at[n],
            device_id=(ctx_at(tx, ty), z), device_id_type=MESH,
        ).wait_recv()

    def s_copy(name, lane):
        if name is None:
            n, (u, v), row, rows = 0, (0, 0), 0, 1024
        else:
            n, (u, v), row, rows = SIB[name], name[1:], (0 if name[0] == "a" else 512), 512
        zp, bk = slot(u, v, lane)
        piece = wfull.at[zp, bk, pl.ds(row, rows)]
        return pltpu.make_async_remote_copy(
            src_ref=piece, dst_ref=piece, send_sem=s_send.at[n], recv_sem=s_recv.at[n],
            device_id=(ctx_at(0, 0, 1), z), device_id_type=MESH,
        )

    def s_start(path, u, v):
        name = (path, u, v) if path == "a" else (path, v, u)
        s_copy(name, k).start()

    def a_ref(s, hop, b, sending):
        off = -s * hop if sending else -s * (hop + 1)
        src = attn.at[(z + off + 2 * NZ) % NZ, b]
        if hop == 3:
            src = src.at[pl.ds(0 if s == 1 else 64, 64)]
        return src

    def a_copy(s, hop, b, sending=True):
        n = (b * 4 + hop) * 2 + (0 if s == 1 else 1)
        ref = a_ref(s, hop, b, sending)
        return pltpu.make_async_remote_copy(
            src_ref=ref, dst_ref=ref, send_sem=a_send.at[n], recv_sem=a_recv.at[n],
            device_id=(c, (z + s + NZ) % NZ), device_id_type=MESH,
        )

    def a_start(hop, b):
        for s in (1, -1):
            if hop:
                a_copy(s, hop - 1, b, False).wait_recv()
            a_copy(s, hop, b).start()

    def kv_sent(i, carry):
        d = (c + i) % NCTX
        kv_copy(d, c).wait_send()
        return carry

    lax.fori_loop(1, NCTX, kv_sent, 0)

    own_zp, own_bk = slot(0, 0)

    pltpu.make_async_copy(w_hbm, wfull.at[own_zp, own_bk], perm_sem.at[1]).wait()
    for s in (1, -1):
        for path in ("a", "b"):
            w_copy((path, 1, 0, s)).start()
    for s in (1, -1):
        for path in ("a", "b"):
            w_copy((path, 3, 0, s)).start()
    s_copy(None, k).start()

    def kv_landed(i, carry):
        src = (c + i) % NCTX
        kv_copy(c, src).wait_recv()
        return carry

    lax.fori_loop(1, NCTX, kv_landed, 0)

    causal = lax.broadcasted_iota(jnp.int32, (BLK, BLK), 1) <= lax.broadcasted_iota(
        jnp.int32, (BLK, BLK), 0
    )
    nt = (((1,), (1,)), ((), ()))

    def attend(b):
        for h in range(GROUP):
            q8[pl.ds(h * BLK, BLK), :] = qv[pl.ds(b * BLK, BLK), pl.ds(h * HD, HD)]
        own_k = skv[pl.ds(b * BLK, BLK), :]
        own_v = svv[pl.ds(b * BLK, BLK), :]
        for h in range(GROUP):
            rows = pl.ds(h * BLK, BLK)
            s_own = lax.dot_general(q8[rows, :], own_k, nt, preferred_element_type=jnp.float32)
            s_own = jnp.where(causal, s_own, -jnp.inf)
            own_scores[rows, :] = s_own
            mx[rows, :] = s_own

        def score_pair(p, carry):
            i0 = meta[2 * NCTX + b * SEL + 2 * p]
            i1 = meta[2 * NCTX + b * SEL + 2 * p + 1]
            keys = jnp.concatenate([income[i0 // 2, i0 % 2, 0], income[i1 // 2, i1 % 2, 0]], axis=0)
            for h in range(GROUP):
                rows = pl.ds(h * BLK, BLK)
                s = lax.dot_general(q8[rows, :], keys, nt, preferred_element_type=jnp.float32)
                scores[p, rows, :] = s
                mx[rows, :] = jnp.maximum(mx[rows, :], jnp.maximum(s[:, :BLK], s[:, BLK:]))
            return carry

        lax.fori_loop(0, PAIRS, score_pair, 0)

        for h in range(GROUP):
            rows = pl.ds(h * BLK, BLK)
            top = jnp.max(mx[rows, :], axis=1, keepdims=True) * EXP_SCALE
            top = jnp.broadcast_to(top, (BLK, BLK))
            mx[rows, :] = top
            w = jnp.exp2(own_scores[rows, :] * EXP_SCALE - top)
            lsum[rows, :] = w
            acc[rows, :] = jnp.dot(
                w.astype(jnp.bfloat16), own_v, preferred_element_type=jnp.float32
            )

        live = meta[2 * NCTX + 2 * SEL + b]

        def value_pair(p, carry):
            i0 = meta[2 * NCTX + b * SEL + 2 * p]
            i1 = meta[2 * NCTX + b * SEL + 2 * p + 1]
            vals = jnp.concatenate([income[i0 // 2, i0 % 2, 1], income[i1 // 2, i1 % 2, 1]], axis=0)
            off0 = jnp.where(2 * p < live, 0.0, 1e30).astype(jnp.float32)
            off1 = jnp.where(2 * p + 1 < live, 0.0, 1e30).astype(jnp.float32)
            for h in range(GROUP):
                rows = pl.ds(h * BLK, BLK)
                top = mx[rows, :]
                s = scores[p, rows, :]
                w0 = jnp.exp2(s[:, :BLK] * EXP_SCALE - (top + off0))
                w1 = jnp.exp2(s[:, BLK:] * EXP_SCALE - (top + off1))
                lsum[rows, :] = lsum[rows, :] + (w0 + w1)
                w = jnp.concatenate([w0.astype(jnp.bfloat16), w1.astype(jnp.bfloat16)], axis=1)
                acc[rows, :] = acc[rows, :] + jnp.dot(w, vals, preferred_element_type=jnp.float32)
            return carry

        lax.fori_loop(0, PAIRS, value_pair, 0)
        for h in range(GROUP):
            rows = pl.ds(h * BLK, BLK)
            total = jnp.sum(lsum[rows, :], axis=1, keepdims=True)
            attn[z, b, :, pl.ds(h * HD, HD)] = (acc[rows, :] / total).astype(jnp.bfloat16)

    attend(0)
    a_start(0, 0)

    for path in ("a", "b"):
        for s in (1, -1):
            w_arrived((path, 1, 0, s))
            w_copy((path, 2, 0, s)).start()
    for path in ("a", "b"):
        for u in (-1, 1):
            for s in (1, -1):
                w_copy((path, 3, u, s)).start()
            s_start(path, u, 0)

    attend(1)
    a_start(0, 1)
    a_start(1, 0)

    def w_far():
        for path in ("a", "b"):
            for s in (1, -1):
                w_arrived((path, 2, 0, s))
        for path in ("a", "b"):
            for s in (1, -1):
                w_copy((path, 3, 2, s)).start()
            s_start(path, 2, 0)

    def w_pass(u):
        for path in ("a", "b"):
            for s in (1, -1):
                w_arrived((path, 3, u, s))
                w_copy((path, 4, u, s)).start()
                s_start(path, u, -s)

    w_pass(0)
    w_far()
    a_start(1, 1)
    a_start(2, 0)
    w_pass(-1)
    a_start(2, 1)
    w_pass(1)
    a_start(3, 0)
    w_pass(2)
    a_start(3, 1)
    for u in (0, -1, 1, 2):
        for path in ("a", "b"):
            for s in (1, -1):
                w_arrived((path, 4, u, s))
            s_start(path, u, 2)

    s_copy(None, 1 - k).wait_recv()
    for name in SIB:
        s_copy(name, 1 - k).wait_recv()
    for b in range(2):
        for s in (1, -1):
            a_copy(s, 3, b, False).wait_recv()

    for bk in range(4):
        def add(zp, total, bk=bk):
            return total + jnp.dot(
                attn[zp].reshape(2 * BLK, GROUP * HD), wfull[zp, bk],
                preferred_element_type=jnp.float32,
            )

        total = lax.fori_loop(0, NZ, add, jnp.zeros((2 * BLK, 256), jnp.float32))
        o_ref[:, pl.ds(bk * 256, 256)] = total.astype(jnp.bfloat16)

    @pl.when(jnp.logical_not(perm_self))
    def _():
        perm_remote.wait_send()

    for name in PLAN:
        w_copy(name).wait_send()
    s_copy(None, k).wait_send()
    for name in SIB:
        s_copy(name, k).wait_send()
    for b in range(2):
        for hop in range(4):
            for s in (1, -1):
                a_copy(s, hop, b).wait_send()


def per_device(
    queries, cache_keys, cache_values, span_keys, span_values, selected, counts, out_weight
):
    c = lax.axis_index("ctx")
    sel = selected.reshape(NCTX, 2, SEL)
    cnt = counts.reshape(NCTX, 2, 1)
    live = lax.broadcasted_iota(jnp.int32, sel.shape, 2) < cnt
    entry = lax.broadcasted_iota(jnp.int32, sel.shape, 1) * SEL + lax.broadcasted_iota(
        jnp.int32, sel.shape, 2
    )
    key = jnp.where(live & ((sel >> 6) == c), entry * CBLK + (sel & (CBLK - 1)), -1)
    first = jnp.min(jnp.where(key < 0, 2 * SEL * CBLK, key), axis=(1, 2))
    last = jnp.max(jnp.maximum(key, 0), axis=(1, 2))
    send = (jnp.stack((first, last), axis=1) & (CBLK - 1)).reshape(2 * NCTX)

    mine = lax.dynamic_slice_in_dim(selected, 2 * c, 2, 0)
    my_cnt = lax.dynamic_slice_in_dim(counts, 2 * c, 2, 0)
    my_live = (lax.broadcasted_iota(jnp.int32, (2, SEL), 1) < my_cnt[:, None]).reshape(2 * SEL)
    owner = (mine >> 6).reshape(2 * SEL)
    order = jnp.arange(2 * SEL, dtype=jnp.int32)
    earlier = (
        (owner[:, None] == owner[None, :]) & my_live[None, :] & (order[None, :] < order[:, None])
    )
    place = owner * 2 + jnp.any(earlier, axis=1).astype(jnp.int32)
    lead = jnp.broadcast_to(place.reshape(2, SEL)[:, :1], (2, SEL)).reshape(2 * SEL)
    place = jnp.where(my_live, place, lead)
    meta = jnp.concatenate((send, place, my_cnt))

    vmem = pltpu.VMEM
    bf16 = jnp.bfloat16
    f32 = jnp.float32
    dma = pltpu.SemaphoreType.DMA
    hbm = pl.BlockSpec(memory_space=pl.ANY)
    return pl.pallas_call(
        body,
        out_shape=jax.ShapeDtypeStruct((2 * BLK, GROUP * HD), bf16),
        in_specs=[pl.BlockSpec(memory_space=pltpu.SMEM)] + [hbm] * 6,
        out_specs=pl.BlockSpec(memory_space=vmem),
        scratch_shapes=[
            vmem((CBLK, BLK, HD), bf16),
            vmem((CBLK, BLK, HD), bf16),
            vmem((2 * BLK, GROUP * HD), bf16),
            vmem((2 * BLK, HD), bf16),
            vmem((2 * BLK, HD), bf16),
            vmem((NCTX, 2, 2, BLK, HD), bf16),
            vmem((NCTX, 2, 2, BLK, HD), bf16),
            vmem((NZ, 4, 1024, 256), bf16),
            vmem((NZ, 2, BLK, GROUP * HD), bf16),
            vmem((GROUP * BLK, HD), bf16),
            vmem((PAIRS, GROUP * BLK, 2 * BLK), f32),
            vmem((GROUP * BLK, BLK), f32),
            vmem((GROUP * BLK, BLK), f32),
            vmem((GROUP * BLK, BLK), f32),
            vmem((GROUP * BLK, HD), f32),
            dma((5,)),
            dma((NCTX,)),
            dma((NCTX,)),
            dma((2,)),
            dma((len(PLAN),)),
            dma((len(PLAN),)),
            dma((len(SIB) + 1,)),
            dma((len(SIB) + 1,)),
            dma((16,)),
            dma((16,)),
        ],
        compiler_params=pltpu.CompilerParams(
            collective_id=0, has_side_effects=True, vmem_limit_bytes=58 * 2**20
        ),
        cost_estimate=pl.CostEstimate(
            flops=8_000_000_000, bytes_accessed=30_000_000, transcendentals=7_000_000
        ),
        name="sparse_attention_projection",
    )(
        meta,
        queries,
        cache_keys.reshape(CBLK, BLK, HD),
        cache_values.reshape(CBLK, BLK, HD),
        span_keys,
        span_values,
        out_weight,
    )


def solution(mesh):
    placed = (
        P("ctx", "head"),
        P("ctx", "head"),
        P("ctx", "head"),
        P("ctx", "head"),
        P("ctx", "head"),
        P(),
        P(),
        P("head", "ctx"),
    )
    return jax.shard_map(
        per_device, mesh=mesh, in_specs=placed, out_specs=P("ctx", "head"), check_vma=False
    )
```

time: 258 us -> 180 us (0.70)
  Pallas kernels: 0 us -> 173 us
  waiting for transfers between devices: 170 us -> 0 us
  matrix products: 25.9 us -> 0 us
  local copies, waits for them, and re-layouts: 25.6 us -> 4.48 us
  between operations: 13.5 us -> 0.07 us
  other arithmetic: 13.4 us -> 1.87 us
  starting transfers between devices: 8.21 us -> 0 us
    pallas_call x0 -> x1, Pallas kernels: none -> 173 us  [per_device(): pl.pallas_call(body, out_shape=jax.ShapeDtypeStruct((2 * BLK, GROUP * HD)...]
    reduce_scatter x1 -> x0, waiting for transfers between devices: 95.2 us -> none  [per_device(): lax.psum_scatter(partial_value, 'head', scatter_dimension=1, tiled=True)]
    all_to_all x1 -> x0, waiting for transfers between devices: 54.9 us -> none  [per_device(): lax.all_to_all(outgoing, 'ctx', split_axis=0, concat_axis=0, tiled=True)]
    dot_general x9 -> x0, matrix products: 25.9 us -> none  [the longest x1 13.7 us: per_device(): jnp.dot(attention, lax.all_gather(out_weight, 'ctx', axis=1, tiled=True),...]
    all_gather x1 -> x0, waiting for transfers between devices: 19.5 us -> none  [per_device(): lax.all_gather(out_weight, 'ctx', axis=1, tiled=True)]
    gather x3 -> x0, local copies, waits for them, and re-layouts: 9.39 us -> none  [the longest x1 3.9 us: per_device(): value_blocks[slot_block]]
    all_to_all x1 -> x0, starting transfers between devices: 7.99 us -> none  [per_device(): lax.all_to_all(outgoing, 'ctx', split_axis=0, concat_axis=0, tiled=True)]
    reduce_sum x6 -> x0, other arithmetic: 6.56 us -> none  [the longest x4 5.59 us: attend(): row_sum = jnp.sum(p_sel, axis=-1) + jnp.sum(p_own, axis=-1)]
  transfers between devices with their start and end apart: 3 -> 0, of which waited for: 3 -> 0; matrix products, arithmetic and copies ran while one was open for 18% -> 0% of each run, Pallas kernels for 0% -> 0%
where the time goes in v1:
time: 180 us; the launch traced here: 179 us
  Pallas kernels  173 us (96%)
  local copies, waits for them, and re-layouts  4.48 us (2%)
  other arithmetic  1.87 us (1%)
    pallas_call x1, Pallas kernels, per_device(): pl.pallas_call(body, out_shape=jax.ShapeDtypeStruct((2 * BLK, GROUP * HD)...  173 us

profile of v1, /device:TPU:3, one launch (start us, length us, event | category | flops | bytes accessed | tf_op | source)
XLA Modules:
  0.0 179.3 jit_solution(3652734430552762506)
XLA Ops:
  0.0 0.7 dynamic_slice.6
  0.7 0.1 iota_compare_fusion.2
  0.8 0.1 lt.53
  0.9 0.8 constant_dynamic-slice_fusion
  1.7 0.1 copy.15
  1.8 0.1 reshape.53
  1.8 0.2 fusion.1
  2.0 0.1 reshape.57
  2.1 0.1 slice_reduce_fusion
  2.3 0.1 broadcast_in_dim.21
  2.3 0.1 reshape.54
  2.4 0.1 iota.40
  2.5 0.7 fusion.2
  3.3 0.1 reduce_min.14
  3.4 0.1 reduce_min.18
  3.5 0.1 reduce_max.14
  3.6 0.1 reduce_max.18
  3.7 0.1 copy.13
  3.8 0.1 and.40
  3.9 0.6 pad_add_fusion.meta
  4.5 172.9 %sparse_attention_projection.1 = bf16[256,1024]{1,0:T(8,128)(2,1)} custom-call(s32[114]{0:T(128)} %pad_add_fusion.meta, bf16[256,1024]{1,0:T(8,128)(2,1)} %q_hbm.1, bf16[64,128,128]{2,1,0:T(8,128)(2,1)} %bitcast.6, bf16[64,128,128]{2,1,0:T(8,128)(2,1)} %bitcast.7, bf16[256,128]{1,0:T(8,128)(2,1)} %sk_hbm.1, bf16[256,128]{1,0:T(8,128)(2,1)} %sv_hbm.1, ...), custom_call_target="tpu_custom_call" | custom-call | flops 8000000000 | bytes 30000000 | tf_op jit(solution)/shard_map/sparse_attention_projection/pallas_call | solution.py:408
  177.4 1.9 %copy.17 = bf16[256,1024]{1,0:T(8,128)(2,1)} copy(bf16[256,1024]{1,0:T(8,128)(2,1)} %sparse_attention_projection.1) | data formatting | bytes 1048576
  (7 shorter events, 0.0 us)

commit v2 on v1

--- a/solution.py
+++ b/solution.py
@@ -57,7 +57,7 @@
 
 def body(
     meta, q_hbm, ck_hbm, cv_hbm, sk_hbm, sv_hbm, w_hbm, o_ref,
-    kc, vc, qv, skv, svv, outgo, income, wfull, attn, q8, scores, own_scores, mx, lsum, acc,
+    kc, vc, qv, skv, svv, outgo, income, wtmp, wfull, attn, q8, scores, own_scores, mx, lsum, acc,
     load_sem, kv_send, kv_recv, perm_sem, w_send, w_recv, s_send, s_recv, a_send, a_recv,
 ):
     c = lax.axis_index("ctx")
@@ -78,11 +78,11 @@
     def ctx_at(dx, dy, dk=0):
         return ((x + dx + NX) % NX) * 8 + ((y + dy + NY) % NY) * 2 + (k + dk) % 2
 
-    pz = c // 4
     pb = (c // 2) % 2
-    perm_to = (4 * ((pz + z) % NZ) + 2 * pb + k, pz)
-    perm_from = (4 * z + 2 * pb + k, (pz - z + NZ) % NZ)
-    perm_self = (pz == z) & (z == 0)
+    in_plane = 4 * ((c // 4 + z) % NZ) + 2 * pb + k
+    in_self = z == 0
+    to_z = (c // 4 - z + NZ) % NZ
+    z_self = to_z == z
 
     barrier = pltpu.get_barrier_semaphore()
 
@@ -94,30 +94,33 @@
     for dz in (1, NZ - 1):
         pl.semaphore_signal(barrier, inc=1, device_id=(c, (z + dz) % NZ), device_id_type=MESH)
 
-    @pl.when(jnp.logical_not(perm_self))
+    @pl.when(jnp.logical_not(z_self))
     def _():
-        pl.semaphore_signal(barrier, inc=1, device_id=perm_to, device_id_type=MESH)
-        pl.semaphore_signal(barrier, inc=1, device_id=perm_from, device_id_type=MESH)
-
-    pl.semaphore_wait(barrier, jnp.where(perm_self, NCTX + 1, NCTX + 3))
+        pl.semaphore_signal(barrier, inc=1, device_id=(c, to_z), device_id_type=MESH)
+
+    pl.semaphore_wait(barrier, jnp.where(z_self, NCTX + 1, NCTX + 2))
 
     def slot(dx, dy, lane=None):
         xy = ((x + dx + NX) % NX) * NY + (y + dy + NY) % NY
         return (xy // 2 - z + NZ) % NZ, 2 * (xy % 2) + (k if lane is None else lane)
 
-    perm_remote = pltpu.make_async_remote_copy(
-        src_ref=w_hbm, dst_ref=wfull.at[z, 2 * pb + k], send_sem=perm_sem.at[0],
-        recv_sem=perm_sem.at[1], device_id=perm_to, device_id_type=MESH,
-    )
-    perm_local = pltpu.make_async_copy(w_hbm, wfull.at[z, 2 * pb + k], perm_sem.at[1])
-
-    @pl.when(perm_self)
-    def _():
-        perm_local.start()
-
-    @pl.when(jnp.logical_not(perm_self))
-    def _():
-        perm_remote.start()
+    move_in = pltpu.make_async_remote_copy(
+        src_ref=w_hbm, dst_ref=wtmp, send_sem=perm_sem.at[0], recv_sem=perm_sem.at[1],
+        device_id=(in_plane, z), device_id_type=MESH,
+    )
+    keep_in = pltpu.make_async_copy(w_hbm, wtmp, perm_sem.at[1])
+    own_piece = wfull.at[z, 2 * pb + k]
+    move_z = pltpu.make_async_remote_copy(
+        src_ref=wtmp, dst_ref=own_piece, send_sem=perm_sem.at[2], recv_sem=perm_sem.at[3],
+        device_id=(c, to_z), device_id_type=MESH,
+    )
+    keep_z = pltpu.make_async_copy(wtmp, own_piece, perm_sem.at[3])
+
+    def either(flag, one, other):
+        pl.when(flag)(one)
+        pl.when(jnp.logical_not(flag))(other)
+
+    either(in_self, keep_in.start, move_in.start)
 
     loads[0].wait()
     loads[1].wait()
@@ -139,6 +142,8 @@
         blk = meta[2 * c + r]
         income[c, r, 0] = kc[blk]
         income[c, r, 1] = vc[blk]
+    keep_in.wait()
+    either(z_self, keep_z.start, move_z.start)
     loads[2].wait()
     loads[3].wait()
     loads[4].wait()
@@ -209,7 +214,7 @@
 
     own_zp, own_bk = slot(0, 0)
 
-    pltpu.make_async_copy(w_hbm, wfull.at[own_zp, own_bk], perm_sem.at[1]).wait()
+    pltpu.make_async_copy(wtmp, wfull.at[own_zp, own_bk], perm_sem.at[3]).wait()
     for s in (1, -1):
         for path in ("a", "b"):
             w_copy((path, 1, 0, s)).start()
@@ -357,9 +362,8 @@
         total = lax.fori_loop(0, NZ, add, jnp.zeros((2 * BLK, 256), jnp.float32))
         o_ref[:, pl.ds(bk * 256, 256)] = total.astype(jnp.bfloat16)
 
-    @pl.when(jnp.logical_not(perm_self))
-    def _():
-        perm_remote.wait_send()
+    pl.when(jnp.logical_not(in_self))(move_in.wait_send)
+    pl.when(jnp.logical_not(z_self))(move_z.wait_send)
 
     for name in PLAN:
         w_copy(name).wait_send()
@@ -418,6 +422,7 @@
             vmem((2 * BLK, HD), bf16),
             vmem((NCTX, 2, 2, BLK, HD), bf16),
             vmem((NCTX, 2, 2, BLK, HD), bf16),
+            vmem((1024, 256), bf16),
             vmem((NZ, 4, 1024, 256), bf16),
             vmem((NZ, 2, BLK, GROUP * HD), bf16),
             vmem((GROUP * BLK, HD), bf16),
@@ -429,7 +434,7 @@
             dma((5,)),
             dma((NCTX,)),
             dma((NCTX,)),
-            dma((2,)),
+            dma((4,)),
             dma((len(PLAN),)),
             dma((len(PLAN),)),
             dma((len(SIB) + 1,)),

time: 180 us -> 154 us (0.86)
  Pallas kernels: 173 us -> 145 us
    pallas_call x1, Pallas kernels: 173 us -> 145 us  [per_device(): pl.pallas_call(body, out_shape=jax.ShapeDtypeStruct((2 * BLK, GROUP * HD)...]
where the time goes in v2:
time: 154 us; the launch traced here: 152 us
  Pallas kernels  145 us (94%)
  local copies, waits for them, and re-layouts  4.48 us (3%)
  other arithmetic  1.87 us (1%)
    pallas_call x1, Pallas kernels, per_device(): pl.pallas_call(body, out_shape=jax.ShapeDtypeStruct((2 * BLK, GROUP * HD)...  145 us

profile of v2, /device:TPU:3, one launch (start us, length us, event | category | flops | bytes accessed | tf_op | source)
XLA Modules:
  0.0 151.5 jit_solution(3738957464800388908)
XLA Ops:
  0.0 0.7 dynamic_slice.6
  0.7 0.1 iota_compare_fusion.2
  0.8 0.1 lt.53
  0.9 0.8 constant_dynamic-slice_fusion
  1.7 0.1 copy.15
  1.8 0.1 reshape.53
  1.8 0.2 fusion.1
  2.0 0.1 reshape.57
  2.1 0.1 slice_reduce_fusion
  2.3 0.1 broadcast_in_dim.21
  2.3 0.1 reshape.54
  2.4 0.1 iota.40
  2.5 0.7 fusion.2
  3.3 0.1 reduce_min.14
  3.4 0.1 reduce_min.18
  3.5 0.1 reduce_max.14
  3.6 0.1 reduce_max.18
  3.7 0.1 copy.13
  3.8 0.1 and.40
  3.9 0.6 pad_add_fusion.meta
  4.5 145.1 %sparse_attention_projection.1 = bf16[256,1024]{1,0:T(8,128)(2,1)} custom-call(s32[114]{0:T(128)} %pad_add_fusion.meta, bf16[256,1024]{1,0:T(8,128)(2,1)} %q_hbm.1, bf16[64,128,128]{2,1,0:T(8,128)(2,1)} %bitcast.6, bf16[64,128,128]{2,1,0:T(8,128)(2,1)} %bitcast.7, bf16[256,128]{1,0:T(8,128)(2,1)} %sk_hbm.1, bf16[256,128]{1,0:T(8,128)(2,1)} %sv_hbm.1, ...), custom_call_target="tpu_custom_call" | custom-call | flops 8000000000 | bytes 30000000 | tf_op jit(solution)/shard_map/sparse_attention_projection/pallas_call | solution.py:412
  149.7 1.9 %copy.17 = bf16[256,1024]{1,0:T(8,128)(2,1)} copy(bf16[256,1024]{1,0:T(8,128)(2,1)} %sparse_attention_projection.1) | data formatting | bytes 1048576
  (7 shorter events, 0.0 us)

commit v3 on v2

--- a/solution.py
+++ b/solution.py
@@ -51,13 +51,13 @@
 for _path in ("a", "b"):
     for _u in range(-1, 3):
         for _v in range(-1, 3):
-            if (_u, _v) != (0, 0):
-                SIB[_path, _u, _v] = len(SIB) + 1
+            SIB[_path, _u, _v] = len(SIB)
 
 
 def body(
     meta, q_hbm, ck_hbm, cv_hbm, sk_hbm, sv_hbm, w_hbm, o_ref,
-    kc, vc, qv, skv, svv, outgo, income, wtmp, wfull, attn, q8, scores, own_scores, mx, lsum, acc,
+    kc, vc, qv, skv, svv, outgo, income_k, income_v, wtmp, wfull, attn, q8, scores, own_scores, mx, lsum, acc,
+    weights, own_weights,
     load_sem, kv_send, kv_recv, perm_sem, w_send, w_recv, s_send, s_recv, a_send, a_recv,
 ):
     c = lax.axis_index("ctx")
@@ -78,11 +78,34 @@
     def ctx_at(dx, dy, dk=0):
         return ((x + dx + NX) % NX) * 8 + ((y + dy + NY) % NY) * 2 + (k + dk) % 2
 
-    pb = (c // 2) % 2
-    in_plane = 4 * ((c // 4 + z) % NZ) + 2 * pb + k
-    in_self = z == 0
-    to_z = (c // 4 - z + NZ) % NZ
-    z_self = to_z == z
+    def flip(n):
+        return n + 1 - 2 * (n % 2)
+
+    def plane_of(path, across, mirrored):
+        n = 4 * (across % 2) + 2 * ((across // 2 + mirrored) % 2) + mirrored
+        return n if path == "a" else flip(n)
+
+    def shift_of(path, plane):
+        n = plane if path == "a" else flip(plane)
+        mirrored = n % 2
+        return 2 * ((n // 2 + mirrored) % 2) + n // 4, mirrored
+
+    def piece_at(path, px, py):
+        across = (px - z // 2 + NX) % NX
+        mirrored = (py // 2 + z % 2) % 2
+        return plane_of(path, across, mirrored), (py % 2 + mirrored) % 2
+
+    in_plane, in_self, to_z, from_z, z_self, place = [], [], [], [], [], []
+    for path in ("a", "b"):
+        across, mirrored = shift_of(path, z)
+        in_plane.append(((x + across) % NX) * 8 + jnp.where(mirrored == 1, 3 - y, y) * 2 + k)
+        in_self.append((across == 0) & (mirrored == 0))
+        sx = (x - across + NX) % NX
+        sy = jnp.where(mirrored == 1, 3 - y, y)
+        to_z.append(2 * sx + sy // 2)
+        place.append(2 * (sy % 2) + k)
+        from_z.append(piece_at(path, x, y)[0])
+        z_self.append(to_z[-1] == z)
 
     barrier = pltpu.get_barrier_semaphore()
 
@@ -94,63 +117,86 @@
     for dz in (1, NZ - 1):
         pl.semaphore_signal(barrier, inc=1, device_id=(c, (z + dz) % NZ), device_id_type=MESH)
 
-    @pl.when(jnp.logical_not(z_self))
-    def _():
-        pl.semaphore_signal(barrier, inc=1, device_id=(c, to_z), device_id_type=MESH)
-
-    pl.semaphore_wait(barrier, jnp.where(z_self, NCTX + 1, NCTX + 2))
-
-    def slot(dx, dy, lane=None):
-        xy = ((x + dx + NX) % NX) * NY + (y + dy + NY) % NY
-        return (xy // 2 - z + NZ) % NZ, 2 * (xy % 2) + (k if lane is None else lane)
-
-    move_in = pltpu.make_async_remote_copy(
-        src_ref=w_hbm, dst_ref=wtmp, send_sem=perm_sem.at[0], recv_sem=perm_sem.at[1],
-        device_id=(in_plane, z), device_id_type=MESH,
-    )
-    keep_in = pltpu.make_async_copy(w_hbm, wtmp, perm_sem.at[1])
-    own_piece = wfull.at[z, 2 * pb + k]
-    move_z = pltpu.make_async_remote_copy(
-        src_ref=wtmp, dst_ref=own_piece, send_sem=perm_sem.at[2], recv_sem=perm_sem.at[3],
-        device_id=(c, to_z), device_id_type=MESH,
-    )
-    keep_z = pltpu.make_async_copy(wtmp, own_piece, perm_sem.at[3])
+    greeters = NCTX + 1
+    for n in range(2):
+        greeters = greeters + jnp.where(z_self[n], 0, 2)
+
+        @pl.when(jnp.logical_not(z_self[n]))
+        def _(n=n):
+            pl.semaphore_signal(barrier, inc=1, device_id=(c, to_z[n]), device_id_type=MESH)
+            pl.semaphore_signal(barrier, inc=1, device_id=(c, from_z[n]), device_id_type=MESH)
+
+    pl.semaphore_wait(barrier, greeters)
+
+    def slot(path, dx, dy, lane=None):
+        zp, b = piece_at(path, (x + dx + NX) % NX, (y + dy + NY) % NY)
+        return zp, 2 * b + (k if lane is None else lane)
+
+    move_in, keep_in, move_z, keep_z = [], [], [], []
+    for n in range(2):
+        half = pl.ds(n * 512, 512)
+        dst = wfull.at[z, place[n], half]
+        sems = [perm_sem.at[4 * n + m] for m in range(4)]
+        move_in.append(pltpu.make_async_remote_copy(
+            src_ref=w_hbm.at[half], dst_ref=wtmp.at[half], send_sem=sems[0], recv_sem=sems[1],
+            device_id=(in_plane[n], z), device_id_type=MESH,
+        ))
+        keep_in.append(pltpu.make_async_copy(w_hbm.at[half], wtmp.at[half], sems[1]))
+        move_z.append(pltpu.make_async_remote_copy(
+            src_ref=wtmp.at[half], dst_ref=dst, send_sem=sems[2], recv_sem=sems[3],
+            device_id=(c, to_z[n]), device_id_type=MESH,
+        ))
+        keep_z.append(pltpu.make_async_copy(wtmp.at[half], dst, sems[3]))
 
     def either(flag, one, other):
         pl.when(flag)(one)
         pl.when(jnp.logical_not(flag))(other)
 
-    either(in_self, keep_in.start, move_in.start)
-
-    loads[0].wait()
-    loads[1].wait()
-
-    def kv_copy(d, source):
+    for n in range(2):
+        either(in_self[n], keep_in[n].start, move_in[n].start)
+
+    income = (income_k, income_v)
+
+    def kv_copy(part, d, source):
         return pltpu.make_async_remote_copy(
-            src_ref=outgo.at[d], dst_ref=income.at[source], send_sem=kv_send.at[d],
-            recv_sem=kv_recv.at[source], device_id=(d, z), device_id_type=MESH,
+            src_ref=outgo.at[part, d], dst_ref=income[part].at[source],
+            send_sem=kv_send.at[part, d], recv_sem=kv_recv.at[part, source],
+            device_id=(d, z), device_id_type=MESH,
         )
 
-    for dx, dy, dk in KV_ORDER:
-        d = ctx_at(dx, dy, dk)
+    for part, cache in enumerate((kc, vc)):
+        loads[part].wait()
+        for dx, dy, dk in KV_ORDER:
+            d = ctx_at(dx, dy, dk)
+            for r in range(2):
+                outgo[part, d, r] = cache[meta[2 * d + r]]
+            kv_copy(part, d, c).start()
         for r in range(2):
-            blk = meta[2 * d + r]
-            outgo[d, r, 0] = kc[blk]
-            outgo[d, r, 1] = vc[blk]
-        kv_copy(d, c).start()
-    for r in range(2):
-        blk = meta[2 * c + r]
-        income[c, r, 0] = kc[blk]
-        income[c, r, 1] = vc[blk]
-    keep_in.wait()
-    either(z_self, keep_z.start, move_z.start)
+            income[part][c, r] = cache[meta[2 * c + r]]
+    for n in range(2):
+        keep_in[n].wait()
+        either(z_self[n], keep_z[n].start, move_z[n].start)
     loads[2].wait()
     loads[3].wait()
     loads[4].wait()
 
+    def kv_landed(part):
+        def one(i, carry):
+            kv_copy(part, c, (c + i) % NCTX).wait_recv()
+            return carry
+
+        lax.fori_loop(1, NCTX, one, 0)
+
+    def kv_sent(part):
+        def one(i, carry):
+            kv_copy(part, (c + i) % NCTX, c).wait_send()
+            return carry
+
+        lax.fori_loop(1, NCTX, one, 0)
+
     def w_copy(name):
         (dx, dy), row, rows, (tx, ty) = PLAN[name]
-        zp, bk = slot(dx, dy)
+        zp, bk = slot(name[0], dx, dy)
         piece = wfull.at[zp, bk, pl.ds(row, rows)]
         n = PLAN_ID[name]
         return pltpu.make_async_remote_copy(
@@ -160,7 +206,7 @@
 
     def w_arrived(name):
         (dx, dy), row, rows, (tx, ty) = PLAN[name]
-        zp, bk = slot(dx - tx, dy - ty)
+        zp, bk = slot(name[0], dx - tx, dy - ty)
         piece = wfull.at[zp, bk, pl.ds(row, rows)]
         n = PLAN_ID[name]
         pltpu.make_async_remote_copy(
@@ -169,11 +215,9 @@
         ).wait_recv()
 
     def s_copy(name, lane):
-        if name is None:
-            n, (u, v), row, rows = 0, (0, 0), 0, 1024
-        else:
-            n, (u, v), row, rows = SIB[name], name[1:], (0 if name[0] == "a" else 512), 512
-        zp, bk = slot(u, v, lane)
+        path, u, v = name
+        n, row, rows = SIB[name], (0 if path == "a" else 512), 512
+        zp, bk = slot(path, u, v, lane)
         piece = wfull.at[zp, bk, pl.ds(row, rows)]
         return pltpu.make_async_remote_copy(
             src_ref=piece, dst_ref=piece, send_sem=s_send.at[n], recv_sem=s_recv.at[n],
@@ -205,98 +249,115 @@
                 a_copy(s, hop - 1, b, False).wait_recv()
             a_copy(s, hop, b).start()
 
-    def kv_sent(i, carry):
-        d = (c + i) % NCTX
-        kv_copy(d, c).wait_send()
-        return carry
-
-    lax.fori_loop(1, NCTX, kv_sent, 0)
-
-    own_zp, own_bk = slot(0, 0)
-
-    pltpu.make_async_copy(wtmp, wfull.at[own_zp, own_bk], perm_sem.at[3]).wait()
-    for s in (1, -1):
+    def w_own():
+        for n, path in enumerate(("a", "b")):
+            zp, bk = slot(path, 0, 0)
+            half = pl.ds(n * 512, 512)
+            pltpu.make_async_copy(wtmp.at[half], wfull.at[zp, bk, half], perm_sem.at[4 * n + 3]).wait()
+        for stage in (1, 3):
+            for s in (1, -1):
+                for path in ("a", "b"):
+                    w_copy((path, stage, 0, s)).start()
         for path in ("a", "b"):
-            w_copy((path, 1, 0, s)).start()
-    for s in (1, -1):
-        for path in ("a", "b"):
-            w_copy((path, 3, 0, s)).start()
-    s_copy(None, k).start()
-
-    def kv_landed(i, carry):
-        src = (c + i) % NCTX
-        kv_copy(c, src).wait_recv()
-        return carry
-
-    lax.fori_loop(1, NCTX, kv_landed, 0)
+            s_start(path, 0, 0)
 
     causal = lax.broadcasted_iota(jnp.int32, (BLK, BLK), 1) <= lax.broadcasted_iota(
         jnp.int32, (BLK, BLK), 0
     )
     nt = (((1,), (1,)), ((), ()))
 
-    def attend(b):
+    def weigh(b):
         for h in range(GROUP):
             q8[pl.ds(h * BLK, BLK), :] = qv[pl.ds(b * BLK, BLK), pl.ds(h * HD, HD)]
         own_k = skv[pl.ds(b * BLK, BLK), :]
+        live = meta[2 * NCTX + 2 * SEL + b]
+        for part in range(2):
+            heads = [(h, pl.ds(h * BLK, BLK), pl.ds((part * 4 + h) * BLK, BLK)) for h in range(4)]
+            for h, rows, all_rows in heads:
+                s_own = lax.dot_general(
+                    q8[all_rows, :], own_k, nt, preferred_element_type=jnp.float32
+                )
+                s_own = jnp.where(causal, s_own, -jnp.inf)
+                own_scores[rows, :] = s_own
+                mx[rows, :] = s_own
+
+            def score_pair(p, carry, heads=heads):
+                i0 = meta[2 * NCTX + b * SEL + 2 * p]
+                i1 = meta[2 * NCTX + b * SEL + 2 * p + 1]
+                keys = jnp.concatenate(
+                    [income_k[i0 // 2, i0 % 2], income_k[i1 // 2, i1 % 2]], axis=0
+                )
+                for h, rows, all_rows in heads:
+                    s = lax.dot_general(
+                        q8[all_rows, :], keys, nt, preferred_element_type=jnp.float32
+                    )
+                    scores[p, rows, :] = s
+                    mx[rows, :] = jnp.maximum(mx[rows, :], jnp.maximum(s[:, :BLK], s[:, BLK:]))
+                return carry
+
+            lax.fori_loop(0, PAIRS, score_pair, 0)
+
+            for h, rows, all_rows in heads:
+                top = jnp.max(mx[rows, :], axis=1, keepdims=True) * EXP_SCALE
+                top = jnp.broadcast_to(top, (BLK, BLK))
+                mx[rows, :] = top
+                w = jnp.exp2(own_scores[rows, :] * EXP_SCALE - top)
+                lsum[b, all_rows, :] = w
+                own_weights[b, all_rows, :] = w.astype(jnp.bfloat16)
+
+            def weight_pair(p, carry, heads=heads):
+                off0 = jnp.where(2 * p < live, 0.0, 1e30).astype(jnp.float32)
+                off1 = jnp.where(2 * p + 1 < live, 0.0, 1e30).astype(jnp.float32)
+                for h, rows, all_rows in heads:
+                    top = mx[rows, :]
+                    s = scores[p, rows, :]
+                    w0 = jnp.exp2(s[:, :BLK] * EXP_SCALE - (top + off0))
+                    w1 = jnp.exp2(s[:, BLK:] * EXP_SCALE - (top + off1))
+                    lsum[b, all_rows, :] = lsum[b, all_rows, :] + (w0 + w1)
+                    weights[b, p, all_rows, :BLK] = w0.astype(jnp.bfloat16)
+                    weights[b, p, all_rows, BLK:] = w1.astype(jnp.bfloat16)
+                return carry
+
+            lax.fori_loop(0, PAIRS, weight_pair, 0)
+
+    def apply(b):
         own_v = svv[pl.ds(b * BLK, BLK), :]
         for h in range(GROUP):
             rows = pl.ds(h * BLK, BLK)
-            s_own = lax.dot_general(q8[rows, :], own_k, nt, preferred_element_type=jnp.float32)
-            s_own = jnp.where(causal, s_own, -jnp.inf)
-            own_scores[rows, :] = s_own
-            mx[rows, :] = s_own
-
-        def score_pair(p, carry):
-            i0 = meta[2 * NCTX + b * SEL + 2 * p]
-            i1 = meta[2 * NCTX + b * SEL + 2 * p + 1]
-            keys = jnp.concatenate([income[i0 // 2, i0 % 2, 0], income[i1 // 2, i1 % 2, 0]], axis=0)
+            acc[rows, :] = jnp.dot(
+                own_weights[b, rows, :], own_v, preferred_element_type=jnp.float32
+            )
+
+        def value_pairs(t, carry):
+            vals = []
+            for m in range(4):
+                i0 = meta[2 * NCTX + b * SEL + 8 * t + 2 * m]
+                i1 = meta[2 * NCTX + b * SEL + 8 * t + 2 * m + 1]
+                vals.append(jnp.concatenate(
+                    [income_v[i0 // 2, i0 % 2], income_v[i1 // 2, i1 % 2]], axis=0
+                ))
             for h in range(GROUP):
                 rows = pl.ds(h * BLK, BLK)
-                s = lax.dot_general(q8[rows, :], keys, nt, preferred_element_type=jnp.float32)
-                scores[p, rows, :] = s
-                mx[rows, :] = jnp.maximum(mx[rows, :], jnp.maximum(s[:, :BLK], s[:, BLK:]))
+                total = acc[rows, :]
+                for m in range(4):
+                    total = total + jnp.dot(
+                        weights[b, 4 * t + m, rows, :], vals[m], preferred_element_type=jnp.float32
+                    )
+                acc[rows, :] = total
             return carry
 
-        lax.fori_loop(0, PAIRS, score_pair, 0)
-
+        lax.fori_loop(0, PAIRS // 4, value_pairs, 0)
         for h in range(GROUP):
             rows = pl.ds(h * BLK, BLK)
-            top = jnp.max(mx[rows, :], axis=1, keepdims=True) * EXP_SCALE
-            top = jnp.broadcast_to(top, (BLK, BLK))
-            mx[rows, :] = top
-            w = jnp.exp2(own_scores[rows, :] * EXP_SCALE - top)
-            lsum[rows, :] = w
-            acc[rows, :] = jnp.dot(
-                w.astype(jnp.bfloat16), own_v, preferred_element_type=jnp.float32
-            )
-
-        live = meta[2 * NCTX + 2 * SEL + b]
-
-        def value_pair(p, carry):
-            i0 = meta[2 * NCTX + b * SEL + 2 * p]
-            i1 = meta[2 * NCTX + b * SEL + 2 * p + 1]
-            vals = jnp.concatenate([income[i0 // 2, i0 % 2, 1], income[i1 // 2, i1 % 2, 1]], axis=0)
-            off0 = jnp.where(2 * p < live, 0.0, 1e30).astype(jnp.float32)
-            off1 = jnp.where(2 * p + 1 < live, 0.0, 1e30).astype(jnp.float32)
-            for h in range(GROUP):
-                rows = pl.ds(h * BLK, BLK)
-                top = mx[rows, :]
-                s = scores[p, rows, :]
-                w0 = jnp.exp2(s[:, :BLK] * EXP_SCALE - (top + off0))
-                w1 = jnp.exp2(s[:, BLK:] * EXP_SCALE - (top + off1))
-                lsum[rows, :] = lsum[rows, :] + (w0 + w1)
-                w = jnp.concatenate([w0.astype(jnp.bfloat16), w1.astype(jnp.bfloat16)], axis=1)
-                acc[rows, :] = acc[rows, :] + jnp.dot(w, vals, preferred_element_type=jnp.float32)
-            return carry
-
-        lax.fori_loop(0, PAIRS, value_pair, 0)
-        for h in range(GROUP):
-            rows = pl.ds(h * BLK, BLK)
-            total = jnp.sum(lsum[rows, :], axis=1, keepdims=True)
+            total = jnp.sum(lsum[b, rows, :], axis=1, keepdims=True)
             attn[z, b, :, pl.ds(h * HD, HD)] = (acc[rows, :] / total).astype(jnp.bfloat16)
 
-    attend(0)
+    kv_landed(0)
+    weigh(0)
+    w_own()
+    weigh(1)
+    kv_landed(1)
+    apply(0)
     a_start(0, 0)
 
     for path in ("a", "b"):
@@ -309,7 +370,7 @@
                 w_copy((path, 3, u, s)).start()
             s_start(path, u, 0)
 
-    attend(1)
+    apply(1)
     a_start(0, 1)
     a_start(1, 0)
 
@@ -345,7 +406,6 @@
                 w_arrived((path, 4, u, s))
             s_start(path, u, 2)
 
-    s_copy(None, 1 - k).wait_recv()
     for name in SIB:
         s_copy(name, 1 - k).wait_recv()
     for b in range(2):
@@ -353,21 +413,22 @@
             a_copy(s, 3, b, False).wait_recv()
 
     for bk in range(4):
-        def add(zp, total, bk=bk):
-            return total + jnp.dot(
+        total = jnp.zeros((2 * BLK, 256), jnp.float32)
+        for zp in range(NZ):
+            total = total + jnp.dot(
                 attn[zp].reshape(2 * BLK, GROUP * HD), wfull[zp, bk],
                 preferred_element_type=jnp.float32,
             )
-
-        total = lax.fori_loop(0, NZ, add, jnp.zeros((2 * BLK, 256), jnp.float32))
         o_ref[:, pl.ds(bk * 256, 256)] = total.astype(jnp.bfloat16)
 
-    pl.when(jnp.logical_not(in_self))(move_in.wait_send)
-    pl.when(jnp.logical_not(z_self))(move_z.wait_send)
+    for n in range(2):
+        pl.when(jnp.logical_not(in_self[n]))(move_in[n].wait_send)
+        pl.when(jnp.logical_not(z_self[n]))(move_z[n].wait_send)
+    kv_sent(0)
+    kv_sent(1)
 
     for name in PLAN:
         w_copy(name).wait_send()
-    s_copy(None, k).wait_send()
     for name in SIB:
         s_copy(name, k).wait_send()
     for b in range(2):
@@ -420,25 +481,28 @@
             vmem((2 * BLK, GROUP * HD), bf16),
             vmem((2 * BLK, HD), bf16),
             vmem((2 * BLK, HD), bf16),
-            vmem((NCTX, 2, 2, BLK, HD), bf16),
-            vmem((NCTX, 2, 2, BLK, HD), bf16),
+            vmem((2, NCTX, 2, BLK, HD), bf16),
+            vmem((NCTX, 2, BLK, HD), bf16),
+            vmem((NCTX, 2, BLK, HD), bf16),
             vmem((1024, 256), bf16),
             vmem((NZ, 4, 1024, 256), bf16),
             vmem((NZ, 2, BLK, GROUP * HD), bf16),
             vmem((GROUP * BLK, HD), bf16),
-            vmem((PAIRS, GROUP * BLK, 2 * BLK), f32),
-            vmem((GROUP * BLK, BLK), f32),
-            vmem((GROUP * BLK, BLK), f32),
-            vmem((GROUP * BLK, BLK), f32),
+            vmem((PAIRS, 4 * BLK, 2 * BLK), f32),
+            vmem((4 * BLK, BLK), f32),
+            vmem((4 * BLK, BLK), f32),
+            vmem((2, GROUP * BLK, BLK), f32),
             vmem((GROUP * BLK, HD), f32),
+            vmem((2, PAIRS, GROUP * BLK, 2 * BLK), bf16),
+            vmem((2, GROUP * BLK, BLK), bf16),
             dma((5,)),
-            dma((NCTX,)),
-            dma((NCTX,)),
-            dma((4,)),
+            dma((2, NCTX)),
+            dma((2, NCTX)),
+            dma((8,)),
             dma((len(PLAN),)),
             dma((len(PLAN),)),
-            dma((len(SIB) + 1,)),
-            dma((len(SIB) + 1,)),
+            dma((len(SIB),)),
+            dma((len(SIB),)),
             dma((16,)),
             dma((16,)),
         ],

time: 154 us -> 128 us (0.83)
  Pallas kernels: 145 us -> 119 us
    pallas_call x1, Pallas kernels: 145 us -> 119 us  [per_device(): pl.pallas_call(body, out_shape=jax.ShapeDtypeStruct((2 * BLK, GROUP * HD)...]
where the time goes in v3:
time: 128 us; the launch traced here: 126 us
  Pallas kernels  119 us (93%)
  local copies, waits for them, and re-layouts  4.48 us (4%)
  other arithmetic  1.87 us (1%)
    pallas_call x1, Pallas kernels, per_device(): pl.pallas_call(body, out_shape=jax.ShapeDtypeStruct((2 * BLK, GROUP * HD)...  119 us

profile of v3, /device:TPU:3, one launch (start us, length us, event | category | flops | bytes accessed | tf_op | source)
XLA Modules:
  0.0 125.7 jit_solution(13323551163513681539)
XLA Ops:
  0.0 0.7 dynamic_slice.6
  0.7 0.1 iota_compare_fusion.2
  0.8 0.1 lt.53
  0.9 0.8 constant_dynamic-slice_fusion
  1.7 0.1 copy.15
  1.8 0.1 reshape.53
  1.8 0.2 fusion.1
  2.0 0.1 reshape.57
  2.1 0.1 slice_reduce_fusion
  2.3 0.1 broadcast_in_dim.21
  2.3 0.1 reshape.54
  2.4 0.1 iota.40
  2.5 0.7 fusion.2
  3.3 0.1 reduce_min.14
  3.4 0.1 reduce_min.18
  3.5 0.1 reduce_max.14
  3.6 0.1 reduce_max.18
  3.7 0.1 copy.13
  3.8 0.1 and.40
  3.9 0.6 pad_add_fusion.meta
  4.5 119.3 %sparse_attention_projection.1 = bf16[256,1024]{1,0:T(8,128)(2,1)} custom-call(s32[114]{0:T(128)} %pad_add_fusion.meta, bf16[256,1024]{1,0:T(8,128)(2,1)} %q_hbm.1, bf16[64,128,128]{2,1,0:T(8,128)(2,1)} %bitcast.6, bf16[64,128,128]{2,1,0:T(8,128)(2,1)} %bitcast.7, bf16[256,128]{1,0:T(8,128)(2,1)} %sk_hbm.1, bf16[256,128]{1,0:T(8,128)(2,1)} %sv_hbm.1, ...), custom_call_target="tpu_custom_call" | custom-call | flops 8000000000 | bytes 30000000 | tf_op jit(solution)/shard_map/sparse_attention_projection/pallas_call | solution.py:473
  123.9 1.9 %copy.17 = bf16[256,1024]{1,0:T(8,128)(2,1)} copy(bf16[256,1024]{1,0:T(8,128)(2,1)} %sparse_attention_projection.1) | data formatting | bytes 1048576
  (7 shorter events, 0.0 us)

commit v4 on v3

--- a/solution.py
+++ b/solution.py
@@ -18,6 +18,7 @@
 NCTX = 32
 CBLK = 64
 PAIRS = SEL // 2
+UNROLL = 3
 MESH = pl.DeviceIdType.MESH
 EXP_SCALE = math.log2(math.e) / math.sqrt(HD)
 
@@ -81,12 +82,16 @@
     def flip(n):
         return n + 1 - 2 * (n % 2)
 
+    def table(n, values):
+        return sum(jnp.where(n == m, v, 0) for m, v in enumerate(values))
+
     def plane_of(path, across, mirrored):
         n = 4 * (across % 2) + 2 * ((across // 2 + mirrored) % 2) + mirrored
-        return n if path == "a" else flip(n)
+        return table(n if path == "a" else flip(n), (0, 1, 7, 4, 2, 5, 3, 6))
 
     def shift_of(path, plane):
-        n = plane if path == "a" else flip(plane)
+        n = table(plane, (0, 1, 4, 6, 3, 5, 7, 2))
+        n = n if path == "a" else flip(n)
         mirrored = n % 2
         return 2 * ((n // 2 + mirrored) % 2) + n // 4, mirrored
 
@@ -281,21 +286,26 @@
                 own_scores[rows, :] = s_own
                 mx[rows, :] = s_own
 
-            def score_pair(p, carry, heads=heads):
-                i0 = meta[2 * NCTX + b * SEL + 2 * p]
-                i1 = meta[2 * NCTX + b * SEL + 2 * p + 1]
-                keys = jnp.concatenate(
-                    [income_k[i0 // 2, i0 % 2], income_k[i1 // 2, i1 % 2]], axis=0
-                )
+            def score_pairs(t, carry, heads=heads):
+                keys = []
+                for m in range(UNROLL):
+                    i0 = meta[2 * NCTX + b * SEL + 2 * (UNROLL * t + m)]
+                    i1 = meta[2 * NCTX + b * SEL + 2 * (UNROLL * t + m) + 1]
+                    keys.append(jnp.concatenate(
+                        [income_k[i0 // 2, i0 % 2], income_k[i1 // 2, i1 % 2]], axis=0
+                    ))
                 for h, rows, all_rows in heads:
-                    s = lax.dot_general(
-                        q8[all_rows, :], keys, nt, preferred_element_type=jnp.float32
-                    )
-                    scores[p, rows, :] = s
-                    mx[rows, :] = jnp.maximum(mx[rows, :], jnp.maximum(s[:, :BLK], s[:, BLK:]))
+                    top = mx[rows, :]
+                    for m in range(UNROLL):
+                        s = lax.dot_general(
+                            q8[all_rows, :], keys[m], nt, preferred_element_type=jnp.float32
+                        )
+                        scores[UNROLL * t + m, rows, :] = s
+                        top = jnp.maximum(top, jnp.maximum(s[:, :BLK], s[:, BLK:]))
+                    mx[rows, :] = top
                 return carry
 
-            lax.fori_loop(0, PAIRS, score_pair, 0)
+            lax.fori_loop(0, PAIRS // UNROLL, score_pairs, 0)
 
             for h, rows, all_rows in heads:
                 top = jnp.max(mx[rows, :], axis=1, keepdims=True) * EXP_SCALE
@@ -305,20 +315,24 @@
                 lsum[b, all_rows, :] = w
                 own_weights[b, all_rows, :] = w.astype(jnp.bfloat16)
 
-            def weight_pair(p, carry, heads=heads):
-                off0 = jnp.where(2 * p < live, 0.0, 1e30).astype(jnp.float32)
-                off1 = jnp.where(2 * p + 1 < live, 0.0, 1e30).astype(jnp.float32)
+            def weight_pairs(t, carry, heads=heads):
                 for h, rows, all_rows in heads:
                     top = mx[rows, :]
-                    s = scores[p, rows, :]
-                    w0 = jnp.exp2(s[:, :BLK] * EXP_SCALE - (top + off0))
-                    w1 = jnp.exp2(s[:, BLK:] * EXP_SCALE - (top + off1))
-                    lsum[b, all_rows, :] = lsum[b, all_rows, :] + (w0 + w1)
-                    weights[b, p, all_rows, :BLK] = w0.astype(jnp.bfloat16)
-                    weights[b, p, all_rows, BLK:] = w1.astype(jnp.bfloat16)
+                    total = lsum[b, all_rows, :]
+                    for m in range(UNROLL):
+                        p = UNROLL * t + m
+                        off0 = jnp.where(2 * p < live, 0.0, 1e30).astype(jnp.float32)
+                        off1 = jnp.where(2 * p + 1 < live, 0.0, 1e30).astype(jnp.float32)
+                        s = scores[p, rows, :]
+                        w0 = jnp.exp2(s[:, :BLK] * EXP_SCALE - (top + off0))
+                        w1 = jnp.exp2(s[:, BLK:] * EXP_SCALE - (top + off1))
+                        total = total + (w0 + w1)
+                        weights[b, p, all_rows, :BLK] = w0.astype(jnp.bfloat16)
+                        weights[b, p, all_rows, BLK:] = w1.astype(jnp.bfloat16)
+                    lsum[b, all_rows, :] = total
                 return carry
 
-            lax.fori_loop(0, PAIRS, weight_pair, 0)
+            lax.fori_loop(0, PAIRS // UNROLL, weight_pairs, 0)
 
     def apply(b):
         own_v = svv[pl.ds(b * BLK, BLK), :]
@@ -408,17 +422,24 @@
 
     for name in SIB:
         s_copy(name, 1 - k).wait_recv()
-    for b in range(2):
-        for s in (1, -1):
-            a_copy(s, 3, b, False).wait_recv()
-
     for bk in range(4):
         total = jnp.zeros((2 * BLK, 256), jnp.float32)
-        for zp in range(NZ):
+        for off in (0, 1, 7, 2, 6, 3, 5):
+            zp = (z + off) % NZ
             total = total + jnp.dot(
                 attn[zp].reshape(2 * BLK, GROUP * HD), wfull[zp, bk],
                 preferred_element_type=jnp.float32,
             )
+        scores[bk, : 2 * BLK, :] = total
+    for b in range(2):
+        for s in (1, -1):
+            a_copy(s, 3, b, False).wait_recv()
+    far = (z + NZ // 2) % NZ
+    for bk in range(4):
+        total = scores[bk, : 2 * BLK, :] + jnp.dot(
+            attn[far].reshape(2 * BLK, GROUP * HD), wfull[far, bk],
+            preferred_element_type=jnp.float32,
+        )
         o_ref[:, pl.ds(bk * 256, 256)] = total.astype(jnp.bfloat16)
 
     for n in range(2):

time: 128 us -> 125 us (0.977)
  Pallas kernels: 119 us -> 117 us
    pallas_call x1, Pallas kernels: 119 us -> 117 us  [per_device(): pl.pallas_call(body, out_shape=jax.ShapeDtypeStruct((2 * BLK, GROUP * HD)...]
where the time goes in v4:
time: 125 us; the launch traced here: 124 us
  Pallas kernels  117 us (94%)
  local copies, waits for them, and re-layouts  4.48 us (4%)
  other arithmetic  1.87 us (1%)
    pallas_call x1, Pallas kernels, per_device(): pl.pallas_call(body, out_shape=jax.ShapeDtypeStruct((2 * BLK, GROUP * HD)...  117 us

profile of v4, /device:TPU:3, one launch (start us, length us, event | category | flops | bytes accessed | tf_op | source)
XLA Modules:
  0.0 123.8 jit_solution(6601766489608626704)
XLA Ops:
  0.0 0.7 dynamic_slice.6
  0.7 0.1 iota_compare_fusion.2
  0.8 0.1 lt.53
  0.9 0.8 constant_dynamic-slice_fusion
  1.7 0.1 copy.15
  1.8 0.1 reshape.53
  1.8 0.2 fusion.1
  2.0 0.1 reshape.57
  2.1 0.1 slice_reduce_fusion
  2.3 0.1 broadcast_in_dim.21
  2.3 0.1 reshape.54
  2.4 0.1 iota.40
  2.5 0.7 fusion.2
  3.3 0.1 reduce_min.14
  3.4 0.1 reduce_min.18
  3.5 0.1 reduce_max.14
  3.6 0.1 reduce_max.18
  3.7 0.1 copy.13
  3.8 0.1 and.40
  3.9 0.6 pad_add_fusion.meta
  4.5 117.4 %sparse_attention_projection.1 = bf16[256,1024]{1,0:T(8,128)(2,1)} custom-call(s32[114]{0:T(128)} %pad_add_fusion.meta, bf16[256,1024]{1,0:T(8,128)(2,1)} %q_hbm.1, bf16[64,128,128]{2,1,0:T(8,128)(2,1)} %bitcast.6, bf16[64,128,128]{2,1,0:T(8,128)(2,1)} %bitcast.7, bf16[256,128]{1,0:T(8,128)(2,1)} %sk_hbm.1, bf16[256,128]{1,0:T(8,128)(2,1)} %sv_hbm.1, ...), custom_call_target="tpu_custom_call" | custom-call | flops 8000000000 | bytes 30000000 | tf_op jit(solution)/shard_map/sparse_attention_projection/pallas_call | solution.py:494
  122.0 1.9 %copy.17 = bf16[256,1024]{1,0:T(8,128)(2,1)} copy(bf16[256,1024]{1,0:T(8,128)(2,1)} %sparse_attention_projection.1) | data formatting | bytes 1048576
  (7 shorter events, 0.0 us)

commit v5 on v4

--- a/solution.py
+++ b/solution.py
@@ -373,6 +373,8 @@
     kv_landed(1)
     apply(0)
     a_start(0, 0)
+    apply(1)
+    a_start(0, 1)
 
     for path in ("a", "b"):
         for s in (1, -1):
@@ -384,8 +386,6 @@
                 w_copy((path, 3, u, s)).start()
             s_start(path, u, 0)
 
-    apply(1)
-    a_start(0, 1)
     a_start(1, 0)
 
     def w_far():

time: 125 us -> 125 us (level)
  no operation moved by 1% of the time
where the time goes in v5:
time: 125 us; the launch traced here: 124 us
  Pallas kernels  117 us (94%)
  local copies, waits for them, and re-layouts  4.48 us (4%)
  other arithmetic  1.87 us (1%)
    pallas_call x1, Pallas kernels, per_device(): pl.pallas_call(body, out_shape=jax.ShapeDtypeStruct((2 * BLK, GROUP * HD)...  117 us

profile of v5, /device:TPU:3, one launch (start us, length us, event | category | flops | bytes accessed | tf_op | source)
XLA Modules:
  0.0 123.6 jit_solution(13215746731948216781)
XLA Ops:
  0.0 0.7 dynamic_slice.6
  0.7 0.1 iota_compare_fusion.2
  0.8 0.1 lt.53
  0.9 0.8 constant_dynamic-slice_fusion
  1.7 0.1 copy.15
  1.8 0.1 reshape.53
  1.8 0.2 fusion.1
  2.0 0.1 reshape.57
  2.1 0.1 slice_reduce_fusion
  2.3 0.1 broadcast_in_dim.21
  2.3 0.1 reshape.54
  2.4 0.1 iota.40
  2.5 0.7 fusion.2
  3.3 0.1 reduce_min.14
  3.4 0.1 reduce_min.18
  3.5 0.1 reduce_max.14
  3.6 0.1 reduce_max.18
  3.7 0.1 copy.13
  3.8 0.1 and.40
  3.9 0.6 pad_add_fusion.meta
  4.5 117.2 %sparse_attention_projection.1 = bf16[256,1024]{1,0:T(8,128)(2,1)} custom-call(s32[114]{0:T(128)} %pad_add_fusion.meta, bf16[256,1024]{1,0:T(8,128)(2,1)} %q_hbm.1, bf16[64,128,128]{2,1,0:T(8,128)(2,1)} %bitcast.6, bf16[64,128,128]{2,1,0:T(8,128)(2,1)} %bitcast.7, bf16[256,128]{1,0:T(8,128)(2,1)} %sk_hbm.1, bf16[256,128]{1,0:T(8,128)(2,1)} %sv_hbm.1, ...), custom_call_target="tpu_custom_call" | custom-call | flops 8000000000 | bytes 30000000 | tf_op jit(solution)/shard_map/sparse_attention_projection/pallas_call | solution.py:494
  121.7 1.9 %copy.17 = bf16[256,1024]{1,0:T(8,128)(2,1)} copy(bf16[256,1024]{1,0:T(8,128)(2,1)} %sparse_attention_projection.1) | data formatting | bytes 1048576
  (7 shorter events, 0.0 us)
